TPU v7x, 32 devices: a whole 2x2x4 slice. The times are simulated.
32 devices in a mesh: frame: 8 (over z, x), patch: 4 (over y, core).
Axes of the slice: x: 2, y: 2, z: 4, core: 2. Of those that a mesh axis runs over, the one named last changes fastest.
Arguments:
- coeffs: float32 [16, 4, 8, 36], P('patch', None, 'frame'), may hold values from -1.8 to 1.8
- shifts: int32 [16, 4, 8, 2], P('patch', None, 'frame'), may hold values from -4 to 4
- pixels: bfloat16 [16, 4, 8, 128, 128], P('patch', None, 'frame'), may hold values from -6 to 6
- pupil_mask: int32 [64, 64], replicated, may hold values from 0 to 1, as said below
- chan_map: int32 [16], replicated, may hold values from 0 to 1, as said below
- intersection: int32 [4, 8], P('patch', 'frame'), may hold values from 4 to 16
Outputs:
- blended: float32 [2, 384, 768], P(None, 'patch', 'frame')
- coeff_grad: float32 [16, 4, 8, 36], P('patch', None, 'frame')
Inputs may be any that keep to these rules, and one draw needn't show every extreme that they name: pupil_mask is 1 exactly on the cells whose centres lie in the disc of diameter 64 about the grid's centre, outside a central disc whose radius in cells is drawn from 8 to 21, and off one row and one column of cells (support vanes) whose positions are drawn from 0 to 63. `chan_map`: every channel is named by exactly 8 slots.
All inputs are finite; a program needn't handle non-finite values.
Results may differ from a plain program's by a relative error of at most 0.0003.
Values may be sent and summed in bfloat16 or wider, within the bound.
A program may use at most 64 MiB of HBM per device.

v0:
```python
import functools
import math

import jax
import jax.numpy as jnp
import ml_dtypes
import numpy as np
from jax import lax
from jax.experimental import pallas as pl
from jax.experimental.pallas import tpu as pltpu
from jax.sharding import PartitionSpec as P

CHANNELS = 2
MARGIN = 16
GAMMA = 0.1
RATIO = 0.35

f32 = jnp.float32
bf16 = jnp.bfloat16


def noll_order(noll_index):
    radial = 0
    remain = noll_index - 1
    while remain > radial:
        radial += 1
        remain -= radial
    azimuth = radial % 2 + 2 * ((remain + (radial + 1) % 2) // 2)
    if noll_index % 2 == 1:
        azimuth = -azimuth
    return (radial, azimuth)


def zernike_basis(mode_count, side):
    pos = (np.arange(side) - (side - 1) / 2.0) / (side / 2.0)
    grid_y = pos[:, None] + np.zeros((1, side))
    grid_x = np.zeros((side, 1)) + pos[None, :]
    radius = np.sqrt(grid_x**2 + grid_y**2)
    angle = np.arctan2(grid_y, grid_x)
    out = []
    for noll_index in range(2, mode_count + 2):
        radial, azimuth = noll_order(noll_index)
        m = abs(azimuth)
        total = np.zeros_like(radius)
        for k in range((radial - m) // 2 + 1):
            factor = math.factorial(radial - k) / (
                math.factorial(k)
                * math.factorial((radial + m) // 2 - k)
                * math.factorial((radial - m) // 2 - k)
            )
            total = total + (-1) ** k * factor * radius ** (radial - 2 * k)
        if azimuth == 0:
            out.append(total * math.sqrt(radial + 1.0))
        elif azimuth > 0:
            out.append(total * math.sqrt(2.0 * (radial + 1.0)) * np.cos(m * angle))
        else:
            out.append(total * math.sqrt(2.0 * (radial + 1.0)) * np.sin(m * angle))
    return np.stack(out)


def np_split(table):
    high = table.astype(np.float32).astype(ml_dtypes.bfloat16)
    low = (table - high.astype(np.float64)).astype(np.float32).astype(ml_dtypes.bfloat16)
    return high, low


def left_form(a):
    return np.block([[a.real, -a.imag], [a.imag, a.real]])


def right_form(a):
    return np.block([[a.real, a.imag], [-a.imag, a.real]])


def half_rows(n):
    return -(-(n // 2 + 1) // 8) * 8


def make_tables(n, margin):
    side = n // 2
    rows = half_rows(n)
    index = np.arange(n)
    full = np.exp(-2j * np.pi * ((index[:, None] * index[None, :]) % n) / n)
    part = full[:, :side]
    dist = np.minimum(index, n - 1 - index)
    taper = np.where(dist < margin, 0.5 - 0.5 * np.cos(np.pi * (dist + 0.5) / margin), 1.0)
    valid = np.arange(rows) <= n // 2
    half = np.where(valid[:, None], full[np.arange(rows) % n], 0.0)
    double = np.where(valid, np.where(np.arange(rows) % (n // 2) == 0, 1.0, 2.0), 0.0)
    tables = {}
    h, l = np_split(right_form(part.T))
    tables["t1a"], tables["t1l"] = np.concatenate([h, h]), l
    h, l = np_split(left_form(part))
    tables["t2a"], tables["t2l"] = np.concatenate([h, h], 1), l
    real_right = np.concatenate([full.T.real, full.T.imag], 1)
    h, l = np_split(real_right)
    tables["taa"], tables["tal"] = np.concatenate([h, h]), l
    h, l = np_split(real_right * taper[:, None])
    tables["tpa"] = np.concatenate([h, l])
    h, l = np_split(left_form(half))
    tables["tb"] = np.concatenate([h, l])
    h, l = np_split(left_form(half * taper[None, :]))
    tables["tbp"] = np.concatenate([h, l])
    h, l = np_split(left_form(half.conj().T * double[None, :]))
    tables["ub"] = np.concatenate([h, l])
    h, l = np_split(np.concatenate([full.real, full.imag]))
    tables["ua"] = np.concatenate([h, l], 1)
    h, l = np_split(left_form(part.conj().T))
    tables["u2"] = np.concatenate([h, l])
    h, l = np_split(right_form(part.conj()))
    tables["u1"] = np.concatenate([h, l], 1)
    return tables


NAMES = ("t1a", "t1l", "t2a", "t2l", "taa", "tal", "tpa", "tb", "tbp", "ub", "ua", "u2", "u1")


def split(x):
    high = x.astype(bf16)
    return high, (x - high.astype(f32)).astype(bf16)


def dot(a, b):
    return jnp.dot(a, b, preferred_element_type=f32)


def rows_cat(*parts):
    return jnp.concatenate(parts, axis=0)


def lanes_cat(*parts):
    return jnp.concatenate(parts, axis=1)


def left_wide(table, high, low):
    m = table.shape[0] // 2
    both = dot(table, high)
    return both[:m] + both[m:] + dot(table[:m], low)


def right_wide(x, table):
    m = table.shape[1] // 2
    high, low = split(x)
    both = dot(high, table)
    return both[:, :m] + both[:, m:] + dot(low, table[:, :m])


def sincos_small(r):
    z = r * r
    s = r + r * z * (-1.6666654611e-1 + z * (8.3321608736e-3 + z * -1.9515295891e-4))
    c = 1.0 - 0.5 * z + z * z * (4.166664568298827e-2 + z * (-1.388731625493765e-3 + z * 2.443315711809948e-5))
    return s, c


def quadrant(s, c, q):
    swap = (q & 1) == 1
    sn = jnp.where(swap, c, s)
    cs = jnp.where(swap, s, c)
    sn = jnp.where((q & 2) == 2, -sn, sn)
    cs = jnp.where(((q + 1) & 2) == 2, -cs, cs)
    return sn, cs


def sincos(x, turn):
    k = jnp.round(x * (2.0 / math.pi))
    r = x - k * 1.5703125
    r = r - k * 4.837512969970703125e-4
    r = r - k * 7.549789948768648e-8
    s, c = sincos_small(r)
    return quadrant(s, c, k.astype(jnp.int32) + turn)


def paired(x, r):
    n = x.shape[1] // 2
    return rows_cat(
        lanes_cat(x[:r, :n], x[r:, :n]), lanes_cat(x[:r, n:], x[r:, n:])
    )


def unpaired(x, r):
    n = x.shape[1] // 2
    return rows_cat(
        lanes_cat(x[:r, :n], x[r:, :n]), lanes_cat(x[:r, n:], x[r:, n:])
    )


def forward_pairs(base, pairs, n, modes, coef, chan, zern, mask, t, q_s, f_s, h_s, inv_s):
    side = n // 2
    hr = half_rows(n)
    count = 2 * pairs
    acc = [jnp.zeros((side, n), f32) for _ in range(count)]
    for j in range(modes):
        z = zern[j]
        for g in range(count):
            acc[g] = acc[g] + coef[base + g, j] * z
    turn = jnp.where(lax.broadcasted_iota(jnp.int32, (side, n), 1) < side, 1, 0)
    pupils = []
    for g in range(count):
        scale = 1.0 / (1.0 + RATIO * jnp.full((1, n), chan[base + g], jnp.int32).astype(f32))
        sn, cs = sincos(acc[g] * scale, turn)
        pupils.append(mask * sn)
        q_s[base + g] = mask * cs * scale
    for p in range(pairs):
        s0 = base + 2 * p
        high, low = split(rows_cat(pupils[2 * p], pupils[2 * p + 1]))
        half = dot(lanes_cat(high, low), t["t1a"][...]) + dot(high, t["t1l"][...])
        high, low = split(paired(half, side))
        field = dot(t["t2a"][...], rows_cat(high, low)) + dot(t["t2l"][...], high)
        f_s[s0] = field[:, :n]
        f_s[s0 + 1] = field[:, n:]
        inten = field[:n] * field[:n] + field[n:] * field[n:]
        inv0 = 1.0 / jnp.sum(inten[:, :n], keepdims=True)
        inv1 = 1.0 / jnp.sum(inten[:, n:], keepdims=True)
        inv_s[s0] = jnp.broadcast_to(inv0, (8, n))
        inv_s[s0 + 1] = jnp.broadcast_to(inv1, (8, n))
        high, low = split(rows_cat(inten[:, :n], inten[:, n:]))
        inner = dot(lanes_cat(high, low), t["taa"][...]) + dot(high, t["tal"][...])
        high, low = split(paired(inner, n))
        otf = left_wide(t["tb"][...], high, low)
        h_s[s0] = otf[:, :n] * inv0
        h_s[s0 + 1] = otf[:, n:] * inv1


def spectrum_pairs(base, pairs, n, pix, shift, chan, t, h_s, s_s, num_s, den_s):
    hr = half_rows(n)
    row = lax.broadcasted_iota(jnp.int32, (hr, n), 0)
    col = lax.broadcasted_iota(jnp.int32, (hr, n), 1)
    num = [[num_s[c, :hr], num_s[c, hr:]] for c in range(CHANNELS)]
    den = [den_s[c] for c in range(CHANNELS)]
    for p in range(pairs):
        s0 = base + 2 * p
        both = rows_cat(pix[s0], pix[s0 + 1])
        inner = dot(lanes_cat(both, both), t["tpa"][...])
        high, low = split(paired(inner, n))
        spec = left_wide(t["tbp"][...], high, low)
        for g in range(2):
            s = s0 + g
            sr = spec[:hr, g * n : (g + 1) * n]
            si = spec[hr:, g * n : (g + 1) * n]
            turns = (row * shift[s, 0] + col * shift[s, 1]) & (n - 1)
            quarter = n // 4
            q = (turns + quarter // 2) // quarter
            rest = (turns - q * quarter).astype(f32) * (2.0 * math.pi / n)
            sn, cs = quadrant(*sincos_small(rest), q)
            vr = sr * cs - si * sn
            vi = sr * sn + si * cs
            s_s[s, :hr] = vr
            s_s[s, hr:] = vi
            hre = h_s[s, :hr]
            him = h_s[s, hr:]
            cr = hre * vr + him * vi
            ci = hre * vi - him * vr
            power = hre * hre + him * him
            for c in range(CHANNELS):
                mine = jnp.full((1, n), chan[s], jnp.int32) == c
                num[c][0] = num[c][0] + jnp.where(mine, cr, 0.0)
                num[c][1] = num[c][1] + jnp.where(mine, ci, 0.0)
                den[c] = den[c] + jnp.where(mine, power, 0.0)
    for c in range(CHANNELS):
        num_s[c, :hr] = num[c][0]
        num_s[c, hr:] = num[c][1]
        den_s[c] = den[c]


def back_transform(left, right, n, t):
    high, low = split(lanes_cat(left, right))
    part = left_wide(t["ub"][...], high, low)
    return right_wide(unpaired(part, n), t["ua"][...])


def backward_pairs(base, pairs, n, modes, chan, zern, t, q_s, f_s, h_s, inv_s, s_s, obj_s, cg_s):
    side = n // 2
    hr = half_rows(n)
    loss = 1.0 / float(n * n * n)
    weights = []
    for p in range(pairs):
        s0 = base + 2 * p
        grads = []
        for g in range(2):
            s = s0 + g
            first = jnp.full((1, n), chan[s], jnp.int32) == 0
            o_re = jnp.where(first, obj_s[0, :hr], obj_s[1, :hr])
            o_im = jnp.where(first, obj_s[0, hr:], obj_s[1, hr:])
            hre = h_s[s, :hr]
            him = h_s[s, hr:]
            rre = s_s[s, :hr] - (o_re * hre - o_im * him)
            rim = s_s[s, hr:] - (o_re * him + o_im * hre)
            grads.append(
                rows_cat(
                    (-2.0 * loss) * (rre * o_re + rim * o_im),
                    (2.0 * loss) * (rre * o_im - rim * o_re),
                )
            )
        psf_grad = back_transform(grads[0], grads[1], n, t)
        field_grads = []
        for g in range(2):
            s = s0 + g
            pg = psf_grad[g * n : (g + 1) * n]
            fr = f_s[s, :n]
            fi = f_s[s, n:]
            inv = inv_s[s][:1]
            mean = inv * jnp.sum(pg * (fr * fr + fi * fi), keepdims=True)
            gi = (2.0 * inv) * (pg - mean)
            field_grads.append(rows_cat(fr * gi, fi * gi))
        high, low = split(lanes_cat(field_grads[0], field_grads[1]))
        part = left_wide(t["u2"][...], high, low)
        pupil_grad = right_wide(unpaired(part, side), t["u1"][...])
        for g in range(2):
            weights.append(q_s[s0 + g] * pupil_grad[g * side : (g + 1) * side])
    pad = cg_s.shape[1]
    for j in range(modes):
        z = zern[j]
        for g in range(2 * pairs):
            cg_s[base + g, j : j + 1] = jnp.sum(z * weights[g], axis=0, keepdims=True)


def window_weight(width, n):
    def ramp(axis):
        pos = lax.broadcasted_iota(jnp.int32, (n, n), axis)
        dist = (jnp.minimum(pos, n - 1 - pos) + 1).astype(f32)
        return jnp.minimum(1.0, dist / (jnp.full((1, n), width, jnp.int32).astype(f32) + 1.0))

    return ramp(0) * ramp(1)


def kernel(n, modes, slots, group, coef, shift, chan, inter, pix, mask_ref, zern, *rest):
    t = dict(zip(NAMES, rest[: len(NAMES)]))
    canvas, grad, q_s, f_s, h_s, inv_s, s_s, num_s, den_s, obj_s, cg_s = rest[len(NAMES) :]
    hr = half_rows(n)
    pairs = group // 2
    m = mask_ref[...].astype(f32)
    mask = lanes_cat(m, m)
    cg_s[...] = jnp.zeros_like(cg_s)
    num_s[...] = jnp.zeros_like(num_s)
    den_s[...] = jnp.zeros_like(den_s)

    @pl.loop(0, slots // group)
    def _(i):
        forward_pairs(i * group, pairs, n, modes, coef, chan, zern, mask, t, q_s, f_s, h_s, inv_s)

    @pl.loop(0, slots // group)
    def _(i):
        spectrum_pairs(i * group, pairs, n, pix, shift, chan, t, h_s, s_s, num_s, den_s)

    for c in range(CHANNELS):
        d = 1.0 / (den_s[c] + GAMMA)
        obj_s[c, :hr] = num_s[c, :hr] * d
        obj_s[c, hr:] = num_s[c, hr:] * d
    images = back_transform(obj_s[0], obj_s[1], n, t) * (1.0 / (n * n))
    weight = window_weight(inter[0, 0], n)
    canvas[0] = images[:n] * weight
    canvas[1] = images[n:] * weight
    canvas[2] = weight

    @pl.loop(0, slots // group)
    def _(i):
        backward_pairs(
            i * group, pairs, n, modes, chan, zern, t, q_s, f_s, h_s, inv_s, s_s, obj_s, cg_s
        )

    flat = cg_s[...].reshape(slots * cg_s.shape[1], n)
    grad[...] = lax.dot_general(
        jnp.ones((8, n), f32), flat, (((1,), (1,)), ((), ())),
        precision=lax.Precision.HIGHEST, preferred_element_type=f32,
    )


def padded(cells, sides, width):
    for axis, dim in sides:
        count = lax.axis_size(axis)
        ends = count - 1
        head = lax.slice_in_dim(cells, 0, width, axis=dim)
        tail = lax.slice_in_dim(cells, cells.shape[dim] - width, cells.shape[dim], axis=dim)
        cells = jnp.concatenate(
            [
                lax.ppermute(tail, axis, [(i, (i + 1) % count) for i in range(ends)]),
                cells,
                lax.ppermute(head, axis, [((i + 1) % count, i) for i in range(ends)]),
            ],
            axis=dim,
        )
    return cells


def fold_margins(extended, axis_num, margin):
    span = extended.shape[axis_num] - 4 * margin
    upper_part = lax.slice_in_dim(extended, 0, margin, axis=axis_num)
    middle = lax.slice_in_dim(extended, 2 * margin, 2 * margin + span, axis=axis_num)
    lower_part = lax.slice_in_dim(extended, span + 3 * margin, span + 4 * margin, axis=axis_num)
    pad_upper = [(0, 0)] * extended.ndim
    pad_lower = [(0, 0)] * extended.ndim
    pad_upper[axis_num] = (0, span - margin)
    pad_lower[axis_num] = (span - margin, 0)
    return middle + jnp.pad(upper_part, pad_upper) + jnp.pad(lower_part, pad_lower)


def per_device(coeffs, shifts, pixels, pupil_mask, chan_map, intersection):
    modes = coeffs.shape[3]
    n = pixels.shape[3]
    margin = MARGIN
    slots = chan_map.shape[0]
    group = 4
    hr = half_rows(n)
    side = n // 2
    pad = -(-modes // 8) * 8
    own_pix = lax.all_to_all(pixels, "patch", split_axis=1, concat_axis=0, tiled=True)
    both = jnp.concatenate([coeffs, shifts.astype(f32)], axis=3)
    both = lax.all_to_all(both, "patch", split_axis=1, concat_axis=0, tiled=True)
    both = both.reshape(slots, modes + 2)
    own_coef = both[:, :modes]
    own_shift = both[:, modes:].astype(jnp.int32)
    z = zernike_basis(modes, side)
    zern = jnp.asarray(np.concatenate([z, z], axis=2).astype(np.float32))
    tables = make_tables(n, margin)
    smem = pl.BlockSpec(memory_space=pltpu.SMEM)
    vmem = pl.BlockSpec(memory_space=pltpu.VMEM)
    canvas, grad = pl.pallas_call(
        functools.partial(kernel, n, modes, slots, group),
        out_shape=(
            jax.ShapeDtypeStruct((CHANNELS + 1, n, n), f32),
            jax.ShapeDtypeStruct((8, slots * pad), f32),
        ),
        in_specs=[smem] * 4 + [vmem] * (3 + len(NAMES)),
        out_specs=(vmem, vmem),
        scratch_shapes=[
            pltpu.VMEM((slots, side, n), f32),
            pltpu.VMEM((slots, 2 * n, n), f32),
            pltpu.VMEM((slots, 2 * hr, n), f32),
            pltpu.VMEM((slots, 8, n), f32),
            pltpu.VMEM((slots, 2 * hr, n), f32),
            pltpu.VMEM((CHANNELS, 2 * hr, n), f32),
            pltpu.VMEM((CHANNELS, hr, n), f32),
            pltpu.VMEM((CHANNELS, 2 * hr, n), f32),
            pltpu.VMEM((slots, pad, n), f32),
        ],
        compiler_params=pltpu.CompilerParams(vmem_limit_bytes=48 * 1024 * 1024),
    )(
        own_coef, own_shift, chan_map, intersection, own_pix.reshape(slots, n, n), pupil_mask, zern,
        *[jnp.asarray(tables[name]) for name in NAMES],
    )
    grad = grad[0].reshape(slots, pad)[:, :modes].reshape(slots, 1, 1, modes)
    coeff_grad = lax.all_to_all(grad, "patch", split_axis=0, concat_axis=1, tiled=True)
    extended = padded(canvas, (("frame", 2), ("patch", 1)), margin)
    folded = fold_margins(fold_margins(extended, 1, margin), 2, margin)
    blended = folded[:CHANNELS] / folded[CHANNELS][None]
    return (blended, coeff_grad)


def solution(mesh):
    in_specs = (
        P("patch", None, "frame", None),
        P("patch", None, "frame", None),
        P("patch", None, "frame", None, None),
        P(),
        P(),
        P("patch", "frame"),
    )
    out_specs = (P(None, "patch", "frame"), P("patch", None, "frame", None))
    return jax.shard_map(
        per_device, mesh=mesh, in_specs=in_specs, out_specs=out_specs, check_vma=False
    )
```

profile of v0, /device:TPU:25, one launch (start us, length us, event | category | flops | bytes accessed | tf_op | source)
XLA Modules:
  0.0 76.8 jit_solution(9292194438872878800)
XLA Ops:
  0.6 0.0 copy-start.4
  0.6 0.0 copy-start.5
  0.7 0.0 copy-start.6
  0.7 0.0 copy-start.1
  0.7 0.0 copy-start.2
  0.7 0.0 copy-start.3
  0.7 0.0 copy-start.11
  0.7 0.0 copy-start
  0.7 0.0 copy-start.15
  0.7 0.0 copy-start.14
  0.8 0.8 %copy_convert_fusion = f32[4,4,1,2]{1,0,3,2:T(4,128)S(1)} fusion(s32[4,4,1,2]{1,3,2,0:T(2,128)} %param.21), kind=kLoop, calls=%fused_computation.12 | loop fusion | flops 32 | bytes 256 | tf_op jit(solution)/shard_map/convert_element_type | solution.py:407
  1.6 0.1 copy.35
  1.7 0.8 %fusion.4 = f32[4,4,1,38]{3,2,1,0:T(1,128)S(1)} fusion(f32[4,4,1,2]{3,2,0,1:T(1,128)S(1)} %copy.35, f32[4,4,1,36]{3,2,1,0:T(1,128)} %param.20), kind=kLoop, calls=%fused_computation.15 | loop fusion | flops 608 | bytes 4864
  2.5 0.5 broadcast.17
  3.0 0.7 reduce.2
  3.7 0.7 reshape.19
  4.4 3.9 %all-to-all-start = ((f32[4,1,152]{2,1,0:T(1,128)}), f32[4,1,152]{2,1,0:T(1,128)S(1)}, u32[]{:S(2)}, u32[]{:S(2)}) async-start(f32[4,1,152]{2,1,0:T(1,128)} %reshape.19), calls=%async_computation | async-start | bytes 8192 | tf_op jit(solution)/shard_map/all_to_all | solution.py:408
  8.2 1.9 %copy.36 = bf16[4,4,1,128,128]{4,3,2,0,1:T(8,128)(2,1)} copy(bf16[4,4,1,128,128]{4,3,2,1,0:T(8,128)(2,1)} %param.22) | data formatting | bytes 1048576 | tf_op args[2]
  10.1 1.2 %all-to-all-done = f32[4,1,152]{2,1,0:T(1,128)S(1)} async-done(((f32[4,1,152]{2,1,0:T(1,128)}), f32[4,1,152]{2,1,0:T(1,128)S(1)}, u32[]{:S(2)}, u32[]{:S(2)}) %all-to-all-start) | async-done | bytes 2464 | tf_op jit(solution)/shard_map/all_to_all | solution.py:408
  11.3 4.1 %all-to-all-start.1 = ((bf16[4,4,1,128,128]{4,3,2,0,1:T(8,128)(2,1)}), bf16[4,4,1,128,128]{4,3,2,0,1:T(8,128)(2,1)S(1)}, u32[]{:S(2)}, u32[]{:S(2)}) async-start(bf16[4,4,1,128,128]{4,3,2,0,1:T(8,128)(2,1)} %copy.36), calls=%async_computation.1 | async-start | bytes 1048576 | tf_op jit(solution)/shard_map/all_to_all | solution.py:406
  16.1 0.7 reduce.3
  16.8 0.1 reshape.20
  16.9 0.1 slice_convert_fusion.shift
  17.0 6.5 %all-to-all-done.1 = bf16[4,4,1,128,128]{4,3,2,0,1:T(8,128)(2,1)S(1)} async-done(((bf16[4,4,1,128,128]{4,3,2,0,1:T(8,128)(2,1)}), bf16[4,4,1,128,128]{4,3,2,0,1:T(8,128)(2,1)S(1)}, u32[]{:S(2)}, u32[]{:S(2)}) %all-to-all-start.1) | async-done | bytes 524320 | tf_op jit(solution)/shard_map/all_to_all | solution.py:406
  23.5 0.0 copy-done.4
  23.5 0.0 copy-done.5
  23.5 0.0 copy-done.6
  23.5 0.0 copy-done.1
  23.5 0.0 copy-done.2
  23.5 0.0 copy-done.3
  23.5 0.0 copy-done.11
  23.5 0.0 copy-done
  23.5 0.0 copy-done.15
  23.5 0.0 copy-done.14
  23.5 0.0 copy-start.7
  23.5 0.9 %copy-done.7 = bf16[256,256]{1,0:T(8,128)(2,1)S(1)} copy-done((bf16[256,256]{1,0:T(8,128)(2,1)S(1)}, bf16[256,256]{1,0:T(8,128)(2,1)}, u32[]{:S(2)}) %copy-start.7) | copy-done | bytes 131096
  24.4 0.9 %copy-done.8 = bf16[256,256]{1,0:T(8,128)(2,1)S(1)} copy-done((bf16[256,256]{1,0:T(8,128)(2,1)S(1)}, bf16[256,256]{1,0:T(8,128)(2,1)}, u32[]{:S(2)}) %copy-start.8) | copy-done | bytes 131096
  25.3 0.9 %copy-done.9 = bf16[256,256]{1,0:T(8,128)(2,1)S(1)} copy-done((bf16[256,256]{1,0:T(8,128)(2,1)S(1)}, bf16[256,256]{1,0:T(8,128)(2,1)}, u32[]{:S(2)}) %copy-start.9) | copy-done | bytes 131096
  26.3 0.9 %copy-done.10 = bf16[256,256]{1,0:T(8,128)(2,1)S(1)} copy-done((bf16[256,256]{1,0:T(8,128)(2,1)S(1)}, bf16[256,256]{1,0:T(8,128)(2,1)}, u32[]{:S(2)}) %copy-start.10) | copy-done | bytes 131096
  27.2 0.8 %copy-done.12 = bf16[256,128]{1,0:T(8,128)(2,1)S(1)} copy-done((bf16[256,128]{1,0:T(8,128)(2,1)S(1)}, bf16[256,128]{1,0:T(8,128)(2,1)}, u32[]{:S(2)}) %copy-start.12) | copy-done | bytes 65560
  28.0 0.8 %copy-done.13 = bf16[128,256]{1,0:T(8,128)(2,1)S(1)} copy-done((bf16[128,256]{1,0:T(8,128)(2,1)S(1)}, bf16[128,256]{1,0:T(8,128)(2,1)}, u32[]{:S(2)}) %copy-start.13) | copy-done | bytes 65560
  28.8 23.8 %shard_map.203 = (f32[3,128,128]{2,1,0:T(8,128)S(1)}, f32[8,640]{1,0:T(8,128)S(1)}) custom-call(f32[16,36]{1,0:T(8,128)S(1)} %bitcast.25, s32[16,2]{1,0:T(8,128)S(1)} %slice_convert_fusion.shift, s32[16]{0:T(128)S(1)} %copy-done.15, s32[1,1]{1,0:T(1,128)S(6)} %copy.41.inter, bf16[16,128,128]{2,1,0:T(8,128)(2,1)S(1)} %bitcast.23, s32[64,64]{1,0:T(8,128)S(1)} %copy-done.14, ...), custom_call_target="tpu_custom_call" | custom-call | tf_op jit(solution)/shard_map/pallas_call | solution.py:417
  52.6 0.1 fusion.3
  52.8 3.1 %collective-permute-start = (f32[3,128,16]{2,1,0:T(8,128)S(1)}, f32[3,128,16]{2,1,0:T(8,128)S(1)}, u32[]{:S(2)}, u32[]{:S(2)}) collective-permute-start(f32[3,128,16]{2,1,0:T(8,128)S(1)} %get-tuple-element.14), channel_id=1, source_target_pairs={{0,4},{4,8},{8,12},{12,16},{16,20},{20,24},{24,28},{1,5},{5,9},{9,... | collective-permute-start | bytes 73736 | tf_op jit(solution)/shard_map/ppermute | solution.py:376
  55.9 3.1 %collective-permute-start.1 = (f32[3,128,16]{2,1,0:T(8,128)S(1)}, f32[3,128,16]{2,1,0:T(8,128)S(1)}, u32[]{:S(2)}, u32[]{:S(2)}) collective-permute-start(f32[3,128,16]{2,1,0:T(8,128)S(1)} %get-tuple-element.15), channel_id=1, source_target_pairs={{4,0},{8,4},{12,8},{16,12},{20,16},{24,20},{28,24},{5,1},{9,5},{13... | collective-permute-start | bytes 73736 | tf_op jit(solution)/shard_map/ppermute | solution.py:378
  59.0 0.1 reshape_squeeze.3
  59.1 0.7 reduce.4
  59.7 0.1 reshape.21
  59.8 6.9 %all_to_all.48 = f32[4,1,144]{2,1,0:T(1,128)S(1)} all-to-all(f32[4,1,144]{2,1,0:T(1,128)S(1)} %reshape.21), channel_id=1, replica_groups=mesh['frame'=8,'patch'=4] {'patch'}, dimensions={0} | all-to-all | bytes 4608 | tf_op jit(solution)/shard_map/all_to_all | solution.py:442
  66.7 0.7 reduce.5
  67.3 0.1 reshape.22
  67.4 0.6 copy.37
  68.0 0.0 collective-permute-done
  68.1 0.0 collective-permute-done.1
  68.1 0.1 pad_maximum_fusion.2
  68.2 2.2 %collective-permute-start.2 = (f32[3,16,160]{2,1,0:T(8,128)S(1)}, f32[3,16,160]{2,1,0:T(8,128)S(1)}, u32[]{:S(2)}, u32[]{:S(2)}) collective-permute-start(f32[3,16,160]{2,1,0:T(8,128)S(1)} %get-tuple-element.12), channel_id=1, source_target_pairs={{0,1},{1,2},{2,3},{4,5},{5,6},{6,7},{8,9},{9,10},{10,11},{12,13},{... | collective-permute-start | bytes 92168 | tf_op jit(solution)/shard_map/ppermute | solution.py:376
  70.4 2.1 %collective-permute-start.3 = (f32[3,16,160]{2,1,0:T(8,128)S(1)}, f32[3,16,160]{2,1,0:T(8,128)S(1)}, u32[]{:S(2)}, u32[]{:S(2)}) collective-permute-start(f32[3,16,160]{2,1,0:T(8,128)S(1)} %get-tuple-element.13), channel_id=1, source_target_pairs={{1,0},{2,1},{3,2},{5,4},{6,5},{7,6},{9,8},{10,9},{11,10},{13,12},{... | collective-permute-start | bytes 92168 | tf_op jit(solution)/shard_map/ppermute | solution.py:378
  72.5 0.2 pad_maximum_fusion
  72.7 0.0 collective-permute-done.2
  72.7 3.1 %collective-permute-done.3 = f32[3,16,160]{2,1,0:T(8,128)S(1)} collective-permute-done((f32[3,16,160]{2,1,0:T(8,128)S(1)}, f32[3,16,160]{2,1,0:T(8,128)S(1)}, u32[]{:S(2)}, u32[]{:S(2)}) %collective-permute-start.3) | collective-permute-done | bytes 30752 | tf_op jit(solution)/shard_map/ppermute | solution.py:378
  75.8 0.1 slice.62
  75.9 0.0 copy-done.16
  76.0 0.1 fusion.2
  76.1 0.7 slice_divide_fusion
  (9 shorter events, 0.1 us)
Async XLA Ops:
  0.6 22.8 %copy-start.4 = (bf16[256,256]{1,0:T(8,128)(2,1)S(1)}, bf16[256,256]{1,0:T(8,128)(2,1)}, u32[]{:S(2)}) copy-start(bf16[256,256]{1,0:T(8,128)(2,1)} %constant.46.clone.rest_12_) | copy-start | bytes 393220
  0.6 22.8 %copy-start.5 = (bf16[256,256]{1,0:T(8,128)(2,1)S(1)}, bf16[256,256]{1,0:T(8,128)(2,1)}, u32[]{:S(2)}) copy-start(bf16[256,256]{1,0:T(8,128)(2,1)} %constant.45.clone.rest_11_) | copy-start | bytes 393220
  0.7 22.8 %copy-start.6 = (bf16[256,256]{1,0:T(8,128)(2,1)S(1)}, bf16[256,256]{1,0:T(8,128)(2,1)}, u32[]{:S(2)}) copy-start(bf16[256,256]{1,0:T(8,128)(2,1)} %constant.44.clone.rest_10_) | copy-start | bytes 393220
  0.7 22.8 %copy-start.1 = (bf16[512,144]{1,0:T(8,128)(2,1)S(1)}, bf16[512,144]{1,0:T(8,128)(2,1)}, u32[]{:S(2)}) copy-start(bf16[512,144]{1,0:T(8,128)(2,1)} %constant.43.clone.rest_9_) | copy-start | bytes 442372
  0.7 22.8 %copy-start.2 = (bf16[288,256]{1,0:T(8,128)(2,1)S(1)}, bf16[288,256]{1,0:T(8,128)(2,1)}, u32[]{:S(2)}) copy-start(bf16[288,256]{1,0:T(8,128)(2,1)} %constant.42.clone.rest_8_) | copy-start | bytes 442372
  0.7 22.8 %copy-start.3 = (bf16[288,256]{1,0:T(8,128)(2,1)S(1)}, bf16[288,256]{1,0:T(8,128)(2,1)}, u32[]{:S(2)}) copy-start(bf16[288,256]{1,0:T(8,128)(2,1)} %constant.41.clone.rest_7_) | copy-start | bytes 442372
  0.7 22.8 %copy-start.11 = (bf16[128,256]{1,0:T(8,128)(2,1)S(1)}, bf16[128,256]{1,0:T(8,128)(2,1)}, u32[]{:S(2)}) copy-start(bf16[128,256]{1,0:T(8,128)(2,1)} %constant.39.clone.rest_5_) | copy-start | bytes 196612
  0.7 22.8 %copy-start = (f32[36,64,128]{2,1,0:T(8,128)S(1)}, f32[36,64,128]{2,1,0:T(8,128)}, u32[]{:S(2)}) copy-start(f32[36,64,128]{2,1,0:T(8,128)} %constant.33.clone.zern) | copy-start | bytes 3538948
  0.7 22.8 %copy-start.15 = (s32[16]{0:T(128)S(1)}, s32[16]{0:T(128)}, u32[]{:S(2)}) copy-start(s32[16]{0:T(128)} %chan.1) | copy-start | bytes 196
  0.7 22.8 %copy-start.14 = (s32[64,64]{1,0:T(8,128)S(1)}, s32[64,64]{1,0:T(8,128)}, u32[]{:S(2)}) copy-start(s32[64,64]{1,0:T(8,128)} %mask_ref.1) | copy-start | bytes 49156
  4.4 7.0 %all-to-all-start = ((f32[4,1,152]{2,1,0:T(1,128)}), f32[4,1,152]{2,1,0:T(1,128)S(1)}, u32[]{:S(2)}, u32[]{:S(2)}) async-start(f32[4,1,152]{2,1,0:T(1,128)} %reshape.19), calls=%async_computation | async-start | bytes 8192 | tf_op jit(solution)/shard_map/all_to_all | solution.py:408
  11.3 12.1 %all-to-all-start.1 = ((bf16[4,4,1,128,128]{4,3,2,0,1:T(8,128)(2,1)}), bf16[4,4,1,128,128]{4,3,2,0,1:T(8,128)(2,1)S(1)}, u32[]{:S(2)}, u32[]{:S(2)}) async-start(bf16[4,4,1,128,128]{4,3,2,0,1:T(8,128)(2,1)} %copy.36), calls=%async_computation.1 | async-start | bytes 1048576 | tf_op jit(solution)/shard_map/all_to_all | solution.py:406
  23.5 0.9 %copy-start.7 = (bf16[256,256]{1,0:T(8,128)(2,1)S(1)}, bf16[256,256]{1,0:T(8,128)(2,1)}, u32[]{:S(2)}) copy-start(bf16[256,256]{1,0:T(8,128)(2,1)} %constant.40.clone.rest_6_) | copy-start | bytes 393220
  24.4 0.9 %copy-start.8 = (bf16[256,256]{1,0:T(8,128)(2,1)S(1)}, bf16[256,256]{1,0:T(8,128)(2,1)}, u32[]{:S(2)}) copy-start(bf16[256,256]{1,0:T(8,128)(2,1)} %constant.38.clone.rest_4_) | copy-start | bytes 393220
  25.3 0.9 %copy-start.9 = (bf16[256,256]{1,0:T(8,128)(2,1)S(1)}, bf16[256,256]{1,0:T(8,128)(2,1)}, u32[]{:S(2)}) copy-start(bf16[256,256]{1,0:T(8,128)(2,1)} %constant.36.clone.rest_2_) | copy-start | bytes 393220
  26.2 0.9 %copy-start.10 = (bf16[256,256]{1,0:T(8,128)(2,1)S(1)}, bf16[256,256]{1,0:T(8,128)(2,1)}, u32[]{:S(2)}) copy-start(bf16[256,256]{1,0:T(8,128)(2,1)} %constant.34.clone.rest_0_) | copy-start | bytes 393220
  27.2 0.8 %copy-start.12 = (bf16[256,128]{1,0:T(8,128)(2,1)S(1)}, bf16[256,128]{1,0:T(8,128)(2,1)}, u32[]{:S(2)}) copy-start(bf16[256,128]{1,0:T(8,128)(2,1)} %constant.37.clone.rest_3_) | copy-start | bytes 196612
  28.0 0.8 %copy-start.13 = (bf16[128,256]{1,0:T(8,128)(2,1)S(1)}, bf16[128,256]{1,0:T(8,128)(2,1)}, u32[]{:S(2)}) copy-start(bf16[128,256]{1,0:T(8,128)(2,1)} %constant.35.clone.rest_1_) | copy-start | bytes 196612
  52.8 15.3 %collective-permute-start = (f32[3,128,16]{2,1,0:T(8,128)S(1)}, f32[3,128,16]{2,1,0:T(8,128)S(1)}, u32[]{:S(2)}, u32[]{:S(2)}) collective-permute-start(f32[3,128,16]{2,1,0:T(8,128)S(1)} %get-tuple-element.14), channel_id=1, source_target_pairs={{0,4},{4,8},{8,12},{12,16},{16,20},{20,24},{24,28},{1,5},{5,9},{9,... | collective-permute-start | bytes 73736 | tf_op jit(solution)/shard_map/ppermute | solution.py:376
  55.9 12.2 %collective-permute-start.1 = (f32[3,128,16]{2,1,0:T(8,128)S(1)}, f32[3,128,16]{2,1,0:T(8,128)S(1)}, u32[]{:S(2)}, u32[]{:S(2)}) collective-permute-start(f32[3,128,16]{2,1,0:T(8,128)S(1)} %get-tuple-element.15), channel_id=1, source_target_pairs={{4,0},{8,4},{12,8},{16,12},{20,16},{24,20},{28,24},{5,1},{9,5},{13... | collective-permute-start | bytes 73736 | tf_op jit(solution)/shard_map/ppermute | solution.py:378
  68.0 7.9 %copy-start.16 = (pred[96]{0:T(512)(128)(4,1)S(1)}, pred[96]{0:T(512)(128)(4,1)}, u32[]{:S(2)}) copy-start(pred[96]{0:T(512)(128)(4,1)} %constant.32.clone.1) | copy-start | bytes 292
  68.2 4.6 %collective-permute-start.2 = (f32[3,16,160]{2,1,0:T(8,128)S(1)}, f32[3,16,160]{2,1,0:T(8,128)S(1)}, u32[]{:S(2)}, u32[]{:S(2)}) collective-permute-start(f32[3,16,160]{2,1,0:T(8,128)S(1)} %get-tuple-element.12), channel_id=1, source_target_pairs={{0,1},{1,2},{2,3},{4,5},{5,6},{6,7},{8,9},{9,10},{10,11},{12,13},{... | collective-permute-start | bytes 92168 | tf_op jit(solution)/shard_map/ppermute | solution.py:376
  70.4 5.4 %collective-permute-start.3 = (f32[3,16,160]{2,1,0:T(8,128)S(1)}, f32[3,16,160]{2,1,0:T(8,128)S(1)}, u32[]{:S(2)}, u32[]{:S(2)}) collective-permute-start(f32[3,16,160]{2,1,0:T(8,128)S(1)} %get-tuple-element.13), channel_id=1, source_target_pairs={{1,0},{2,1},{3,2},{5,4},{6,5},{7,6},{9,8},{10,9},{11,10},{13,12},{... | collective-permute-start | bytes 92168 | tf_op jit(solution)/shard_map/ppermute | solution.py:378
where the time goes:
time: 77.4 us; the launch traced here: 76.8 us
  Pallas kernels  23.8 us (31%)
  starting transfers between devices  18.5 us (24%)
  waiting for transfers between devices  10.8 us (14%)
  local copies, waits for them, and re-layouts  9.75 us (13%)
  blocking collectives  6.87 us (9%)
  other arithmetic  5.52 us (7%)
  between operations  1.57 us (2%)
    pallas_call x1, Pallas kernels, per_device(): pl.pallas_call(functools.partial(kernel, n, modes, slots, group), out_sha...  23.8 us
    unnamed x41, local copies, waits for them, and re-layouts  9.3 us
    all_to_all x1, blocking collectives, per_device(): lax.all_to_all(grad, 'patch', split_axis=0, concat_axis=1, tiled=True)  6.87 us
    all_to_all x1, waiting for transfers between devices, per_device(): lax.all_to_all(pixels, 'patch', split_axis=1, concat_axis=0, tiled=True)  6.49 us
    ppermute x2, starting transfers between devices, padded(): lax.ppermute(tail, axis, [(i, (i + 1) % count) for i in range(ends)])  5.34 us
    ppermute x2, starting transfers between devices, padded(): lax.ppermute(head, axis, [((i + 1) % count, i) for i in range(ends)])  5.16 us
    all_to_all x1, starting transfers between devices, per_device(): lax.all_to_all(pixels, 'patch', split_axis=1, concat_axis=0, tiled=True)  4.14 us
    all_to_all x1, starting transfers between devices, per_device(): lax.all_to_all(both, 'patch', split_axis=1, concat_axis=0, tiled=True)  3.89 us
  transfers between devices with their start and end apart: 6, of which 3 were waited for; matrix products, arithmetic and copies ran while one was open for 7% of the time, Pallas kernels for 0%

commit v1 on v0

--- a/solution.py
+++ b/solution.py
@@ -113,6 +113,18 @@
 
 
 NAMES = ("t1a", "t1l", "t2a", "t2l", "taa", "tal", "tpa", "tb", "tbp", "ub", "ua", "u2", "u1")
+MESH = pl.DeviceIdType.MESH
+
+
+def pack_tables(n, margin):
+    tables = make_tables(n, margin)
+    places, blocks, at = {}, [], 0
+    for name in NAMES:
+        block = tables[name]
+        places[name] = (at, block.shape[0], block.shape[1])
+        blocks.append(np.pad(block, ((0, 0), (0, 2 * n - block.shape[1]))))
+        at += block.shape[0]
+    return np.concatenate(blocks), places
 
 
 def split(x):
@@ -189,10 +201,11 @@
     hr = half_rows(n)
     count = 2 * pairs
     acc = [jnp.zeros((side, n), f32) for _ in range(count)]
+    rows = [coef[base + g] for g in range(count)]
     for j in range(modes):
         z = zern[j]
         for g in range(count):
-            acc[g] = acc[g] + coef[base + g, j] * z
+            acc[g] = acc[g] + rows[g][:, j : j + 1] * z
     turn = jnp.where(lax.broadcasted_iota(jnp.int32, (side, n), 1) < side, 1, 0)
     pupils = []
     for g in range(count):
@@ -203,9 +216,9 @@
     for p in range(pairs):
         s0 = base + 2 * p
         high, low = split(rows_cat(pupils[2 * p], pupils[2 * p + 1]))
-        half = dot(lanes_cat(high, low), t["t1a"][...]) + dot(high, t["t1l"][...])
+        half = dot(lanes_cat(high, low), t("t1a")) + dot(high, t("t1l"))
         high, low = split(paired(half, side))
-        field = dot(t["t2a"][...], rows_cat(high, low)) + dot(t["t2l"][...], high)
+        field = dot(t("t2a"), rows_cat(high, low)) + dot(t("t2l"), high)
         f_s[s0] = field[:, :n]
         f_s[s0 + 1] = field[:, n:]
         inten = field[:n] * field[:n] + field[n:] * field[n:]
@@ -214,9 +227,9 @@
         inv_s[s0] = jnp.broadcast_to(inv0, (8, n))
         inv_s[s0 + 1] = jnp.broadcast_to(inv1, (8, n))
         high, low = split(rows_cat(inten[:, :n], inten[:, n:]))
-        inner = dot(lanes_cat(high, low), t["taa"][...]) + dot(high, t["tal"][...])
+        inner = dot(lanes_cat(high, low), t("taa")) + dot(high, t("tal"))
         high, low = split(paired(inner, n))
-        otf = left_wide(t["tb"][...], high, low)
+        otf = left_wide(t("tb"), high, low)
         h_s[s0] = otf[:, :n] * inv0
         h_s[s0 + 1] = otf[:, n:] * inv1
 
@@ -230,14 +243,15 @@
     for p in range(pairs):
         s0 = base + 2 * p
         both = rows_cat(pix[s0], pix[s0 + 1])
-        inner = dot(lanes_cat(both, both), t["tpa"][...])
+        inner = dot(lanes_cat(both, both), t("tpa"))
         high, low = split(paired(inner, n))
-        spec = left_wide(t["tbp"][...], high, low)
+        spec = left_wide(t("tbp"), high, low)
         for g in range(2):
             s = s0 + g
             sr = spec[:hr, g * n : (g + 1) * n]
             si = spec[hr:, g * n : (g + 1) * n]
-            turns = (row * shift[s, 0] + col * shift[s, 1]) & (n - 1)
+            move = shift[s]
+            turns = (row * move[:, 0:1] + col * move[:, 1:2]) & (n - 1)
             quarter = n // 4
             q = (turns + quarter // 2) // quarter
             rest = (turns - q * quarter).astype(f32) * (2.0 * math.pi / n)
@@ -264,8 +278,8 @@
 
 def back_transform(left, right, n, t):
     high, low = split(lanes_cat(left, right))
-    part = left_wide(t["ub"][...], high, low)
-    return right_wide(unpaired(part, n), t["ua"][...])
+    part = left_wide(t("ub"), high, low)
+    return right_wide(unpaired(part, n), t("ua"))
 
 
 def backward_pairs(base, pairs, n, modes, chan, zern, t, q_s, f_s, h_s, inv_s, s_s, obj_s, cg_s):
@@ -303,8 +317,8 @@
             gi = (2.0 * inv) * (pg - mean)
             field_grads.append(rows_cat(fr * gi, fi * gi))
         high, low = split(lanes_cat(field_grads[0], field_grads[1]))
-        part = left_wide(t["u2"][...], high, low)
-        pupil_grad = right_wide(unpaired(part, side), t["u1"][...])
+        part = left_wide(t("u2"), high, low)
+        pupil_grad = right_wide(unpaired(part, side), t("u1"))
         for g in range(2):
             weights.append(q_s[s0 + g] * pupil_grad[g * side : (g + 1) * side])
     pad = cg_s.shape[1]
@@ -323,22 +337,126 @@
     return ramp(0) * ramp(1)
 
 
-def kernel(n, modes, slots, group, coef, shift, chan, inter, pix, mask_ref, zern, *rest):
-    t = dict(zip(NAMES, rest[: len(NAMES)]))
-    canvas, grad, q_s, f_s, h_s, inv_s, s_s, num_s, den_s, obj_s, cg_s = rest[len(NAMES) :]
+def kernel(
+    n, modes, slots, group, places, margin,
+    chan, inter, coeffs, shifts, mask_ref, pix_in, zern_in, tab_in,
+    blended, grad_out,
+    q_s, f_s, h_s, inv_s, s_s, num_s, den_s, obj_s, cg_s,
+    pix, zern, tab, coef, shift, canvas, strips, landed, part_s, back_s,
+    load_sem, c_send, c_recv, s_send, s_recv, p_send, p_recv, m_send, m_recv, g_send, g_recv,
+):
+    peers = lax.axis_size("patch")
+    cols = lax.axis_size("frame")
+    me = lax.axis_index("patch")
+    col = lax.axis_index("frame")
+    local = slots // peers
     hr = half_rows(n)
     pairs = group // 2
-    m = mask_ref[...].astype(f32)
-    mask = lanes_cat(m, m)
+    steps = slots // group
+
+    def t(name):
+        at, r, c = places[name]
+        return tab[at : at + r, :c]
+
+    load_zern = pltpu.make_async_copy(zern_in, zern, load_sem.at[0])
+    load_tab = pltpu.make_async_copy(tab_in, tab, load_sem.at[1])
+    load_pix = pltpu.make_async_copy(pix_in.at[:, me], pix.at[pl.ds(me * local, local)], load_sem.at[2])
+    load_zern.start()
+    load_tab.start()
+    load_pix.start()
+
+    sides = []
+    for dr in (-1, 0, 1):
+        for dc in (-1, 0, 1):
+            if dr == 0 and dc == 0:
+                continue
+            strip = {(-1): 0, 1: 1}[dr] if dr else {(-1): 2, 1: 3}[dc]
+            place = len(sides)
+            sides.append((dr, dc, strip, place))
+
+    def exists(dr, dc):
+        ok = (me + dr >= 0) & (me + dr < peers)
+        return ok & (col + dc >= 0) & (col + dc < cols)
+
+    landed[...] = jnp.zeros_like(landed)
+
+    barrier = pltpu.get_barrier_semaphore()
+    for k in range(1, peers):
+        pl.semaphore_signal(
+            barrier, inc=1, device_id=(col, lax.rem(me + k, peers)), device_id_type=MESH
+        )
+    expected = jnp.int32(peers - 1)
+    for dr, dc, strip, place in sides:
+        if dc == 0:
+            continue
+        ok = exists(dr, dc)
+        expected = expected + jnp.where(ok, 1, 0)
+
+        @pl.when(ok)
+        def _():
+            pl.semaphore_signal(
+                barrier, inc=1, device_id=(col + dc, me + dr), device_id_type=MESH
+            )
+
     cg_s[...] = jnp.zeros_like(cg_s)
     num_s[...] = jnp.zeros_like(num_s)
     den_s[...] = jnp.zeros_like(den_s)
-
-    @pl.loop(0, slots // group)
+    coef[pl.ds(me * local, local)] = coeffs[:, me]
+    shift[pl.ds(me * local, local)] = shifts[:, me]
+    m = mask_ref[...].astype(f32)
+    mask = lanes_cat(m, m)
+    pl.semaphore_wait(barrier, expected)
+
+    def remote(src, dst, send, recv, k, to):
+        return pltpu.make_async_remote_copy(
+            src_ref=src, dst_ref=dst, send_sem=send.at[k], recv_sem=recv.at[k],
+            device_id=to, device_id_type=MESH,
+        )
+
+    sends = []
+    for k in range(1, peers):
+        to = lax.rem(me + k, peers)
+        mine = pl.ds(me * local, local)
+        device = (col, to)
+        sends.append(remote(coeffs.at[:, to], coef.at[mine], c_send, c_recv, k, device))
+        sends.append(remote(shifts.at[:, to], shift.at[mine], s_send, s_recv, k, device))
+    for k in range(1, peers):
+        to = lax.rem(me + k, peers)
+        sends.append(
+            remote(pix_in.at[:, to], pix.at[pl.ds(me * local, local)], p_send, p_recv, k, (col, to))
+        )
+    for send in sends:
+        send.start()
+
+    def arrived(src, dst, send, recv, k):
+        origin = lax.rem(me + peers - k, peers)
+        return remote(src.at[:, me], dst.at[pl.ds(origin * local, local)], send, recv, k, (col, origin))
+
+    load_zern.wait()
+    load_tab.wait()
+    own_first = local % group == 0
+    first = me * local // group if own_first else 0
+
+    def wait_coef():
+        for k in range(1, peers):
+            arrived(coeffs, coef, c_send, c_recv, k).wait_recv()
+
+    if not own_first:
+        wait_coef()
+
+    @pl.loop(0, steps)
     def _(i):
-        forward_pairs(i * group, pairs, n, modes, coef, chan, zern, mask, t, q_s, f_s, h_s, inv_s)
-
-    @pl.loop(0, slots // group)
+        if own_first and peers > 1:
+            pl.when(i == local // group)(wait_coef)
+        base = lax.rem(first + i, steps) * group
+        forward_pairs(base, pairs, n, modes, coef, chan, zern, mask, t, q_s, f_s, h_s, inv_s)
+
+    load_pix.wait()
+    for k in range(1, peers):
+        arrived(shifts, shift, s_send, s_recv, k).wait_recv()
+        arrived(pix_in, pix, p_send, p_recv, k).wait_recv()
+
+    @pl.loop(0, steps)
     def _(i):
         spectrum_pairs(i * group, pairs, n, pix, shift, chan, t, h_s, s_s, num_s, den_s)
 
@@ -348,54 +466,104 @@
         obj_s[c, hr:] = num_s[c, hr:] * d
     images = back_transform(obj_s[0], obj_s[1], n, t) * (1.0 / (n * n))
     weight = window_weight(inter[0, 0], n)
-    canvas[0] = images[:n] * weight
-    canvas[1] = images[n:] * weight
-    canvas[2] = weight
-
-    @pl.loop(0, slots // group)
+    layers = (images[:n] * weight, images[n:] * weight, weight)
+    for c, layer in enumerate(layers):
+        canvas[c] = layer
+        turned = layer.T
+        strips[0, c] = layer[:margin]
+        strips[1, c] = layer[n - margin :]
+        strips[2, c] = turned[:margin]
+        strips[3, c] = turned[n - margin :]
+
+    def margin_copy(dr, dc, strip, place):
+        there = len(sides) - 1 - place
+        return pltpu.make_async_remote_copy(
+            src_ref=strips.at[strip], dst_ref=landed.at[there],
+            send_sem=m_send.at[place], recv_sem=m_recv.at[there],
+            device_id=(col + dc, me + dr), device_id_type=MESH,
+        )
+
+    def margin_landed(dr, dc, strip, place):
+        return pltpu.make_async_remote_copy(
+            src_ref=strips.at[strip], dst_ref=landed.at[place],
+            send_sem=m_send.at[place], recv_sem=m_recv.at[place],
+            device_id=(col + dc, me + dr), device_id_type=MESH,
+        )
+
+    for side in sides:
+        @pl.when(exists(side[0], side[1]))
+        def _():
+            margin_copy(*side).start()
+
+    @pl.loop(0, steps)
     def _(i):
         backward_pairs(
             i * group, pairs, n, modes, chan, zern, t, q_s, f_s, h_s, inv_s, s_s, obj_s, cg_s
         )
 
-    flat = cg_s[...].reshape(slots * cg_s.shape[1], n)
-    grad[...] = lax.dot_general(
+    pad = cg_s.shape[1]
+    flat = cg_s[...].reshape(slots * pad, n)
+    sums = lax.dot_general(
         jnp.ones((8, n), f32), flat, (((1,), (1,)), ((), ())),
         precision=lax.Precision.HIGHEST, preferred_element_type=f32,
     )
-
-
-def padded(cells, sides, width):
-    for axis, dim in sides:
-        count = lax.axis_size(axis)
-        ends = count - 1
-        head = lax.slice_in_dim(cells, 0, width, axis=dim)
-        tail = lax.slice_in_dim(cells, cells.shape[dim] - width, cells.shape[dim], axis=dim)
-        cells = jnp.concatenate(
-            [
-                lax.ppermute(tail, axis, [(i, (i + 1) % count) for i in range(ends)]),
-                cells,
-                lax.ppermute(head, axis, [((i + 1) % count, i) for i in range(ends)]),
-            ],
-            axis=dim,
+    for s in range(slots):
+        part_s[s] = sums[0:1, s * pad : s * pad + modes]
+    back = []
+    for k in range(1, peers):
+        to = lax.rem(me + k, peers)
+        back.append(
+            remote(part_s.at[pl.ds(to * local, local)], back_s.at[:, me], g_send, g_recv, k, (col, to))
         )
-    return cells
-
-
-def fold_margins(extended, axis_num, margin):
-    span = extended.shape[axis_num] - 4 * margin
-    upper_part = lax.slice_in_dim(extended, 0, margin, axis=axis_num)
-    middle = lax.slice_in_dim(extended, 2 * margin, 2 * margin + span, axis=axis_num)
-    lower_part = lax.slice_in_dim(extended, span + 3 * margin, span + 4 * margin, axis=axis_num)
-    pad_upper = [(0, 0)] * extended.ndim
-    pad_lower = [(0, 0)] * extended.ndim
-    pad_upper[axis_num] = (0, span - margin)
-    pad_lower[axis_num] = (span - margin, 0)
-    return middle + jnp.pad(upper_part, pad_upper) + jnp.pad(lower_part, pad_lower)
+    for send in back:
+        send.start()
+    back_s[:, me] = part_s[pl.ds(me * local, local)]
+
+    for side in sides:
+        @pl.when(exists(side[0], side[1]))
+        def _():
+            margin_landed(*side).wait_recv()
+
+    where = {(dr, dc): place for dr, dc, strip, place in sides}
+    lane = lax.broadcasted_iota(jnp.int32, (margin, n), 1)
+    near = (lane >= margin) & (lane < 2 * margin)
+    far = (lane >= n - 2 * margin) & (lane < n - margin)
+    gap = jnp.zeros((margin, n), f32)
+    wide = jnp.zeros((n - 4 * margin, n), f32)
+    folded = []
+    for c in range(CHANNELS + 1):
+        def edge(dr):
+            corner_l = pltpu.roll(landed[where[dr, -1], c], 2 * margin, 1)
+            corner_r = pltpu.roll(landed[where[dr, 1], c], n - 2 * margin, 1)
+            return (
+                landed[where[dr, 0], c]
+                + jnp.where(near, corner_l, 0.0)
+                + jnp.where(far, corner_r, 0.0)
+            )
+
+        turned = rows_cat(gap, landed[where[0, -1], c], wide, landed[where[0, 1], c], gap)
+        rows = rows_cat(gap, edge(-1), wide, edge(1), gap)
+        folded.append(canvas[c] + turned.T + rows)
+    inverse = 1.0 / folded[CHANNELS][margin : n - margin, margin : n - margin]
+    for c in range(CHANNELS):
+        blended[c] = folded[c][margin : n - margin, margin : n - margin] * inverse
+
+    for k in range(1, peers):
+        origin = lax.rem(me + peers - k, peers)
+        remote(
+            part_s.at[pl.ds(me * local, local)], back_s.at[:, origin], g_send, g_recv, k, (col, origin)
+        ).wait_recv()
+    grad_out[...] = back_s[...]
+    for send in sends + back:
+        send.wait_send()
+    for side in sides:
+        @pl.when(exists(side[0], side[1]))
+        def _():
+            margin_copy(*side).wait_send()
 
 
 def per_device(coeffs, shifts, pixels, pupil_mask, chan_map, intersection):
-    modes = coeffs.shape[3]
+    local, rows, _, modes = coeffs.shape
     n = pixels.shape[3]
     margin = MARGIN
     slots = chan_map.shape[0]
@@ -403,24 +571,22 @@
     hr = half_rows(n)
     side = n // 2
     pad = -(-modes // 8) * 8
-    own_pix = lax.all_to_all(pixels, "patch", split_axis=1, concat_axis=0, tiled=True)
-    both = jnp.concatenate([coeffs, shifts.astype(f32)], axis=3)
-    both = lax.all_to_all(both, "patch", split_axis=1, concat_axis=0, tiled=True)
-    both = both.reshape(slots, modes + 2)
-    own_coef = both[:, :modes]
-    own_shift = both[:, modes:].astype(jnp.int32)
+    peers = lax.axis_size("patch")
     z = zernike_basis(modes, side)
-    zern = jnp.asarray(np.concatenate([z, z], axis=2).astype(np.float32))
-    tables = make_tables(n, margin)
+    zern = np.concatenate([z, z], axis=2).astype(np.float32)
+    tables, places = pack_tables(n, margin)
+    tile = n - 2 * margin
     smem = pl.BlockSpec(memory_space=pltpu.SMEM)
     vmem = pl.BlockSpec(memory_space=pltpu.VMEM)
-    canvas, grad = pl.pallas_call(
-        functools.partial(kernel, n, modes, slots, group),
+    anywhere = pl.BlockSpec(memory_space=pl.ANY)
+    dma = pltpu.SemaphoreType.DMA
+    blended, grad = pl.pallas_call(
+        functools.partial(kernel, n, modes, slots, group, places, margin),
         out_shape=(
-            jax.ShapeDtypeStruct((CHANNELS + 1, n, n), f32),
-            jax.ShapeDtypeStruct((8, slots * pad), f32),
+            jax.ShapeDtypeStruct((CHANNELS, tile, tile), f32),
+            jax.ShapeDtypeStruct((local, rows, 1, modes), f32),
         ),
-        in_specs=[smem] * 4 + [vmem] * (3 + len(NAMES)),
+        in_specs=[smem] * 2 + [vmem] * 3 + [anywhere] * 3,
         out_specs=(vmem, vmem),
         scratch_shapes=[
             pltpu.VMEM((slots, side, n), f32),
@@ -432,18 +598,29 @@
             pltpu.VMEM((CHANNELS, hr, n), f32),
             pltpu.VMEM((CHANNELS, 2 * hr, n), f32),
             pltpu.VMEM((slots, pad, n), f32),
-        ],
-        compiler_params=pltpu.CompilerParams(vmem_limit_bytes=48 * 1024 * 1024),
+            pltpu.VMEM((slots, n, n), bf16),
+            pltpu.VMEM(zern.shape, f32),
+            pltpu.VMEM(tables.shape, bf16),
+            pltpu.VMEM((slots, 1, modes), f32),
+            pltpu.VMEM((slots, 1, 2), jnp.int32),
+            pltpu.VMEM((CHANNELS + 1, n, n), f32),
+            pltpu.VMEM((4, CHANNELS + 1, margin, n), f32),
+            pltpu.VMEM((8, CHANNELS + 1, margin, n), f32),
+            pltpu.VMEM((slots, 1, modes), f32),
+            pltpu.VMEM((local, rows, 1, modes), f32),
+            dma((3,)),
+        ]
+        + [dma((peers,))] * 6
+        + [dma((8,))] * 2
+        + [dma((peers,))] * 2,
+        compiler_params=pltpu.CompilerParams(
+            vmem_limit_bytes=48 * 1024 * 1024, collective_id=0, has_side_effects=True
+        ),
     )(
-        own_coef, own_shift, chan_map, intersection, own_pix.reshape(slots, n, n), pupil_mask, zern,
-        *[jnp.asarray(tables[name]) for name in NAMES],
+        chan_map, intersection, coeffs, shifts, pupil_mask,
+        pixels.reshape(local, rows, n, n), jnp.asarray(zern), jnp.asarray(tables),
     )
-    grad = grad[0].reshape(slots, pad)[:, :modes].reshape(slots, 1, 1, modes)
-    coeff_grad = lax.all_to_all(grad, "patch", split_axis=0, concat_axis=1, tiled=True)
-    extended = padded(canvas, (("frame", 2), ("patch", 1)), margin)
-    folded = fold_margins(fold_margins(extended, 1, margin), 2, margin)
-    blended = folded[:CHANNELS] / folded[CHANNELS][None]
-    return (blended, coeff_grad)
+    return (blended, grad)
 
 
 def solution(mesh):

time: 77.4 us -> 40.5 us (0.52)
  the two profiles are of different devices: /device:TPU:25 before, /device:TPU:0 now
where the time goes in v1:
time: 40.5 us; the launch traced here: 40.2 us
  Pallas kernels  31 us (77%)
  local copies, waits for them, and re-layouts  7.92 us (20%)
  between operations  1.29 us (3%)
    pallas_call x1, Pallas kernels, per_device(): pl.pallas_call(functools.partial(kernel, n, modes, slots, group, places,...  31 us
    unnamed x15, local copies, waits for them, and re-layouts  7.92 us

profile of v1, /device:TPU:0, one launch (start us, length us, event | category | flops | bytes accessed | tf_op | source)
XLA Modules:
  0.0 40.2 jit_solution(13563455712238188792)
XLA Ops:
  1.3 0.8 %copy.10.shifts = s32[4,4,1,2]{3,2,1,0:T(1,128)S(1)} copy(s32[4,4,1,2]{1,3,2,0:T(2,128)} %param.9) | data formatting | bytes 256 | tf_op args[1]
  2.1 0.0 copy-start
  2.1 1.5 %copy-done = bf16[3392,256]{1,0:T(8,128)(2,1)S(1)} copy-done((bf16[3392,256]{1,0:T(8,128)(2,1)S(1)}, bf16[3392,256]{1,0:T(8,128)(2,1)}, u32[]{:S(2)}) %copy-start) | copy-done | bytes 1736728
  3.5 0.0 copy-start.1
  3.5 1.3 %copy-done.1 = f32[36,64,128]{2,1,0:T(8,128)S(1)} copy-done((f32[36,64,128]{2,1,0:T(8,128)S(1)}, f32[36,64,128]{2,1,0:T(8,128)}, u32[]{:S(2)}) %copy-start.1) | copy-done | bytes 1179672
  4.8 0.0 copy-start.2
  4.8 1.0 %copy-done.2 = bf16[4,4,1,128,128]{4,3,2,1,0:T(8,128)(2,1)S(1)} copy-done((bf16[4,4,1,128,128]{4,3,2,1,0:T(8,128)(2,1)S(1)}, bf16[4,4,1,128,128]{4,3,2,1,0:T(8,128)(2,1)}, u32[]{:S(2)}) %copy-start.2) | copy-done | bytes 524312
  5.8 0.0 copy-start.3
  5.8 0.8 %copy-done.3 = s32[64,64]{1,0:T(8,128)S(1)} copy-done((s32[64,64]{1,0:T(8,128)S(1)}, s32[64,64]{1,0:T(8,128)}, u32[]{:S(2)}) %copy-start.3) | copy-done | bytes 16408
  6.6 0.0 copy-start.4
  6.6 0.7 %copy-done.4 = f32[4,4,1,36]{3,2,1,0:T(1,128)S(1)} copy-done((f32[4,4,1,36]{3,2,1,0:T(1,128)S(1)}, f32[4,4,1,36]{3,2,1,0:T(1,128)}, u32[]{:S(2)}) %copy-start.4) | copy-done | bytes 2328
  7.3 0.0 copy-start.5
  7.3 0.7 %copy-done.5 = s32[16]{0:T(128)S(1)} copy-done((s32[16]{0:T(128)S(1)}, s32[16]{0:T(128)}, u32[]{:S(2)}) %copy-start.5) | copy-done | bytes 88
  8.0 31.0 %shard_map.95 = (f32[2,96,96]{2,1,0:T(8,128)S(1)}, f32[4,4,1,36]{3,2,1,0:T(1,128)S(1)}) custom-call(s32[16]{0:T(128)S(1)} %copy-done.5, s32[1,1]{1,0:T(1,128)S(6)} %copy.13.inter, f32[4,4,1,36]{3,2,1,0:T(1,128)S(1)} %copy-done.4, s32[4,4,1,2]{3,2,1,0:T(1,128)S(1)} %copy.10.shifts, s32[64,64]{1,0:T(8,128)S(1)} %copy-done.3, ...), custom_call_target="tpu_custom_call" | custom-call | tf_op jit(solution)/shard_map/pallas_call | solution.py:583
  38.9 0.6 %copy.14 = f32[2,96,96]{2,1,0:T(8,128)} copy(f32[2,96,96]{2,1,0:T(8,128)S(1)} %get-tuple-element.4) | data formatting | bytes 147456
  39.6 0.6 %copy.15 = f32[4,4,1,36]{3,2,1,0:T(1,128)} copy(f32[4,4,1,36]{3,2,1,0:T(1,128)S(1)} %get-tuple-element.5) | data formatting | bytes 4608
Async XLA Ops:
  2.1 1.5 %copy-start = (bf16[3392,256]{1,0:T(8,128)(2,1)S(1)}, bf16[3392,256]{1,0:T(8,128)(2,1)}, u32[]{:S(2)}) copy-start(bf16[3392,256]{1,0:T(8,128)(2,1)} %constant.5.clone.tab_in) | copy-start | bytes 5210116
  3.5 1.3 %copy-start.1 = (f32[36,64,128]{2,1,0:T(8,128)S(1)}, f32[36,64,128]{2,1,0:T(8,128)}, u32[]{:S(2)}) copy-start(f32[36,64,128]{2,1,0:T(8,128)} %constant.4.clone.zern_in) | copy-start | bytes 3538948
  4.8 1.0 %copy-start.2 = (bf16[4,4,1,128,128]{4,3,2,1,0:T(8,128)(2,1)S(1)}, bf16[4,4,1,128,128]{4,3,2,1,0:T(8,128)(2,1)}, u32[]{:S(2)}) copy-start(bf16[4,4,1,128,128]{4,3,2,1,0:T(8,128)(2,1)} %param.10) | copy-start | bytes 1572868
  5.8 0.8 %copy-start.3 = (s32[64,64]{1,0:T(8,128)S(1)}, s32[64,64]{1,0:T(8,128)}, u32[]{:S(2)}) copy-start(s32[64,64]{1,0:T(8,128)} %mask_ref.1) | copy-start | bytes 49156
  6.6 0.7 %copy-start.4 = (f32[4,4,1,36]{3,2,1,0:T(1,128)S(1)}, f32[4,4,1,36]{3,2,1,0:T(1,128)}, u32[]{:S(2)}) copy-start(f32[4,4,1,36]{3,2,1,0:T(1,128)} %coeffs.1) | copy-start | bytes 6916
  7.3 0.7 %copy-start.5 = (s32[16]{0:T(128)S(1)}, s32[16]{0:T(128)}, u32[]{:S(2)}) copy-start(s32[16]{0:T(128)} %chan.1) | copy-start | bytes 196
